TPU v7x, 32 devices: a whole 2x2x4 slice. The times are simulated.
32 devices in a mesh: ia: 4 (over y, x), ja: 2 (over core), ka: 4 (over z).
Axes of the slice: x: 2, y: 2, z: 4, core: 2. Of those that a mesh axis runs over, the one named last changes fastest.
Arguments:
- tensor: bfloat16 [4096, 32, 4096], P('ia', 'ka', 'ja'), may hold values from -64 to 64
- factor_j: bfloat16 [4096, 128], P('ja'), may hold values from -0.0640625 to 0.0640625
- factor_k: bfloat16 [32, 128], P('ka'), may hold values from -0.72478445 to 0.72478445
Outputs:
- core: float32 [128, 32, 4096], P('ia', 'ka', 'ja')
All inputs are finite; a program needn't handle non-finite values.
Results may differ from a plain program's by a relative error of at most 0.013.
Values may be sent and summed in bfloat16 or wider, within the bound.
A program may use at most 128 MiB of HBM per device.

v0:
```python
import jax
import jax.numpy as jnp
from jax import lax
from jax.sharding import PartitionSpec as P


def local_sketch(tensor, factor_j, factor_k):
    rows, slices, columns = tensor.shape
    mixed = jnp.dot(
        tensor.reshape(rows * slices, columns), factor_j, preferred_element_type=jnp.float32
    )
    mixed = mixed.reshape(rows, slices, factor_j.shape[1])
    return jnp.sum(mixed * factor_k.astype(jnp.float32)[None], axis=1)


def local_gram(basis):
    return jnp.dot(
        basis.T, basis, precision=lax.Precision.HIGHEST, preferred_element_type=jnp.float32
    )


def apply_factor(gram, basis):
    lower = jnp.linalg.cholesky(gram)
    return jax.scipy.linalg.solve_triangular(lower, basis.T, lower=True).T


def shards(tensor, factor_j, factor_k):
    rows, slices, columns = tensor.shape
    partial_value = local_sketch(tensor, factor_j, factor_k)
    basis = lax.psum(partial_value, ("ja", "ka"))
    for sweep in range(2):
        gram = lax.psum(local_gram(basis), "ia")
        basis = apply_factor(gram, basis)
    basis_half = basis.astype(jnp.bfloat16)
    flattened = tensor.reshape(rows, slices * columns)
    width = basis_half.shape[1]
    kept_rows = width // lax.axis_size("ia")
    core = lax.psum_scatter(
        lax.dot_general(
            basis_half, flattened, (((0,), (0,)), ((), ())), preferred_element_type=jnp.float32
        ).astype(jnp.bfloat16),
        "ia",
        scatter_dimension=0,
        tiled=True,
    ).astype(jnp.float32)
    return core.reshape(kept_rows, slices, columns)


def solution(mesh):
    return jax.shard_map(
        shards,
        mesh=mesh,
        in_specs=(P("ia", "ka", "ja"), P("ja", None), P("ka", None)),
        out_specs=P("ia", "ka", "ja"),
        check_vma=False,
    )
```

profile of v0, /device:TPU:0, one launch (start us, length us, event | category | flops | bytes accessed | tf_op | source)
XLA Modules:
  0.0 300.6 jit_solution(7561206188565948169)
XLA Ops:
  6.5 0.7 convert_element_type.11
  7.3 0.3 copy-done
  7.6 14.7 %fusion.3 = f32[1024,8,128]{2,1,0:T(8,128)S(1)} fusion(bf16[1024,8,2048]{2,1,0:T(8,128)(2,1)} %param.6, bf16[2048,128]{1,0:T(8,128)(2,1)S(1)} %copy-done), kind=kOutput, calls=%fused_computation.6 | convolution fusion | flops 4294967296 | bytes 38273024 | tf_op jit(solution)/shard_map/dot_general | solution.py:9
  22.3 1.4 fusion
  23.7 0.0 all-reduce.4.cloned.1.call-update
  23.7 0.0 all-reduce.6.cloned.1.call-start
  23.8 58.9 %all-reduce.4.cloned.1.call-done = f32[1024,128]{1,0:T(8,128)} async-done(((f32[1024,128]{1,0:T(8,128)}), f32[1024,128]{1,0:T(8,128)}) %all-reduce.4.cloned.1.call-update) | async-done | bytes 524304 | tf_op jit(solution)/shard_map/psum | solution.py:30
  82.7 2.8 fusion.13
  85.5 0.0 all-reduce.6.cloned.1.call-update
  85.6 0.2 all-reduce.8.cloned.1.call-start
  85.8 40.5 %all-reduce.6.cloned.1.call-done = f32[128,128]{0,1:T(8,128)} async-done(((f32[128,128]{0,1:T(8,128)}), f32[128,128]{0,1:T(8,128)}) %all-reduce.6.cloned.1.call-update) | async-done | bytes 65552 | tf_op jit(solution)/shard_map/psum | solution.py:32
  126.3 0.9 copy.6
  127.2 0.9 fusion.10
  128.1 11.7 %cholesky.44 = f32[128,128]{1,0:T(8,128)S(1)} custom-call(f32[128,128]{1,0:T(8,128)S(1)} %fusion.10), custom_call_target="Cholesky" | custom-call | tf_op jit(solution)/shard_map/jit(cholesky)/cholesky | solution.py:23
  139.8 0.6 compare_reduce_fusion.1
  140.5 0.7 fusion.5
  141.2 9.8 %custom-call.6 = f32[1,128,128]{1,2,0:T(8,128)S(1)} custom-call(f32[1,128,128]{2,1,0:T(8,128)S(1)} %fusion.5), custom_call_target="InvertDiagBlocksLowerTriangular" | custom-call | tf_op jit(solution)/shard_map/jit(_solve_triangular)/triangular_solve | solution.py:24
  151.0 1.7 fusion.1
  152.7 1.2 fusion.14
  153.9 0.0 reduce-scatter.2.cloned.1.call-start
  154.0 30.1 %copy.13 = bf16[128,8,8,2048]{3,1,2,0:T(8,128)(2,1)} copy(bf16[128,8,8,2048]{3,2,1,0:T(8,128)(2,1)} %bitcast.37) | data formatting | bytes 67108864
  184.0 11.5 %all-reduce.8.cloned.1.call-done = f32[128,128]{0,1:T(8,128)} async-done(((f32[128,128]{0,1:T(8,128)}), f32[128,128]{0,1:T(8,128)}) %all-reduce.8.cloned.1.call-update) | async-done | bytes 65552 | tf_op jit(solution)/shard_map/psum | solution.py:32
  195.6 0.9 copy.8
  196.5 0.9 fusion.8
  197.3 11.7 %cholesky.55 = f32[128,128]{1,0:T(8,128)S(1)} custom-call(f32[128,128]{1,0:T(8,128)S(1)} %fusion.8), custom_call_target="Cholesky" | custom-call | tf_op jit(solution)/shard_map/jit(cholesky)/cholesky | solution.py:23
  209.1 0.6 compare_reduce_fusion
  209.7 0.7 fusion.6
  210.4 9.8 %custom-call.7 = f32[1,128,128]{1,2,0:T(8,128)S(1)} custom-call(f32[1,128,128]{2,1,0:T(8,128)S(1)} %fusion.6), custom_call_target="InvertDiagBlocksLowerTriangular" | custom-call | tf_op jit(solution)/shard_map/jit(_solve_triangular)/triangular_solve | solution.py:24
  220.2 0.6 convolution_convert_fusion.1
  220.9 17.2 %convolution_convert_fusion = bf16[128,16384]{1,0:T(8,128)(2,1)} fusion(bf16[128,1024]{1,0:T(8,128)(2,1)S(1)} %convolution_convert_fusion.1, bf16[1024,16384]{1,0:T(8,128)(2,1)} %bitcast.38), kind=kOutput, calls=%fused_computation | convolution fusion | flops 4297064448 | bytes 38010880 | tf_op jit(solution)/shard_map/dot_general | solution.py:39
  238.1 52.9 %reduce-scatter.2.cloned.1.call-done = bf16[32,16384]{1,0:T(8,128)(2,1)} async-done(((bf16[128,16384]{1,0:T(8,128)(2,1)}), bf16[32,16384]{1,0:T(8,128)(2,1)}) %reduce-scatter.2.cloned.1.call-update) | async-done | bytes 1048592 | tf_op jit(solution)/shard_map/reduce_scatter | solution.py:38
  290.9 3.2 %copy.14 = f32[4,8,8,2048]{3,2,1,0:T(8,128)} copy(bf16[4,8,8,2048]{3,1,2,0:T(8,128)(2,1)} %bitcast.39) | data formatting | bytes 3145728
  (8 shorter events, 0.1 us)
Async XLA Ops:
  6.5 1.1 copy-start
  6.5 76.2 %all-reduce.4.cloned.1.call-start = ((), (), s32[]{:S(2)}) async-start(), calls=%async_computation.1 | async-start | bytes 1048576 | tf_op jit(solution)/shard_map/psum | solution.py:30
  23.7 102.6 %all-reduce.6.cloned.1.call-start = ((), (), s32[]{:S(2)}) async-start(), calls=%async_computation.2 | async-start | bytes 131072 | tf_op jit(solution)/shard_map/psum | solution.py:32
  85.6 110.0 %all-reduce.8.cloned.1.call-start = ((), (), s32[]{:S(2)}) async-start(), calls=%async_computation.3 | async-start | bytes 131072 | tf_op jit(solution)/shard_map/psum | solution.py:32
  153.9 137.0 %reduce-scatter.2.cloned.1.call-start = ((), (), s32[]{:S(2)}) async-start(), calls=%async_computation.4 | async-start | bytes 5242880 | tf_op jit(solution)/shard_map/reduce_scatter | solution.py:38
  220.8 73.3 %copy-start.1 = (bf16[2048,128]{1,0:T(8,128)(2,1)S(1)}, bf16[2048,128]{1,0:T(8,128)(2,1)}, u32[]{:S(2)}) copy-start(bf16[2048,128]{1,0:T(8,128)(2,1)} %param.7) | copy-start | bytes 1572868
Sparse Core Ops, SparseCore 0:
  23.8 58.8 all-reduce.3
  85.8 40.4 all-reduce.5
  154.0 41.4 all-reduce.7
  238.2 52.6 reduce-scatter.1
where the time goes:
time: 301 us
  waiting for transfers between devices  164 us (54%)
  other arithmetic  49.5 us (16%)
  matrix products  38.2 us (13%)
  local copies, waits for them, and re-layouts  35.4 us (12%)
  between operations  13.2 us (4%)
    psum x1, waiting for transfers between devices, shards(): basis = lax.psum(partial_value, ('ja', 'ka'))  58.9 us
    reduce_scatter x1, waiting for transfers between devices, shards(): lax.psum_scatter(lax.dot_general(basis_half, flattened, (((0,), (0,)), ((...  52.9 us
    psum x2, waiting for transfers between devices, shards(): gram = lax.psum(local_gram(basis), 'ia')  52.1 us
    unnamed x6, local copies, waits for them, and re-layouts  33.5 us
    another operation x6, other arithmetic, apply_factor(): lower = jnp.linalg.cholesky(gram)  24.8 us
    another operation x4, other arithmetic, apply_factor(): return jax.scipy.linalg.solve_triangular(lower, basis.T, lower=True).T  20.9 us
    dot_general x1, matrix products, shards(): lax.dot_general(basis_half, flattened, (((0,), (0,)), ((), ())), preferre...  17.2 us
    dot_general x1, matrix products, local_sketch(): jnp.dot(tensor.reshape(rows * slices, columns), factor_j, preferred_eleme...  14.7 us
  transfers between devices with their start and end apart: 4, of which 4 were waited for; matrix products, arithmetic and copies ran while one was open for 10% of the time, Pallas kernels for 0%

commit v1 on v0

--- a/solution.py
+++ b/solution.py
@@ -27,7 +27,7 @@
 def shards(tensor, factor_j, factor_k):
     rows, slices, columns = tensor.shape
     partial_value = local_sketch(tensor, factor_j, factor_k)
-    basis = lax.psum(partial_value, ("ja", "ka"))
+    basis = lax.psum(lax.psum(partial_value, "ka"), "ja")
     for sweep in range(2):
         gram = lax.psum(local_gram(basis), "ia")
         basis = apply_factor(gram, basis)

time: 301 us -> 307 us (1.020)
  waiting for transfers between devices: 164 us -> 169 us
    psum x1 -> x2, waiting for transfers between devices: 58.9 us -> 62.1 us  [shards(): basis = lax.psum(lax.psum(partial_value, 'ka'), 'ja')]
  transfers between devices with their start and end apart: 4 -> 5, of which waited for: 4 -> 5; matrix products, arithmetic and copies ran while one was open for 10% -> 10% of each run, Pallas kernels for 0% -> 0%
where the time goes in v1:
time: 307 us; the launch traced here: 306 us
  waiting for transfers between devices  169 us (55%)
  other arithmetic  49.5 us (16%)
  matrix products  38.2 us (12%)
  local copies, waits for them, and re-layouts  35.4 us (12%)
  between operations  13.2 us (4%)
    psum x2, waiting for transfers between devices, shards(): basis = lax.psum(lax.psum(partial_value, 'ka'), 'ja')  62.1 us
    psum x2, waiting for transfers between devices, shards(): gram = lax.psum(local_gram(basis), 'ia')  54.3 us
    reduce_scatter x1, waiting for transfers between devices, shards(): lax.psum_scatter(lax.dot_general(basis_half, flattened, (((0,), (0,)), ((...  52.9 us
    unnamed x6, local copies, waits for them, and re-layouts  33.5 us
    another operation x6, other arithmetic, apply_factor(): lower = jnp.linalg.cholesky(gram)  24.8 us
    another operation x4, other arithmetic, apply_factor(): return jax.scipy.linalg.solve_triangular(lower, basis.T, lower=True).T  20.9 us
    dot_general x1, matrix products, shards(): lax.dot_general(basis_half, flattened, (((0,), (0,)), ((), ())), preferre...  17.2 us
    dot_general x1, matrix products, local_sketch(): jnp.dot(tensor.reshape(rows * slices, columns), factor_j, preferred_eleme...  14.7 us
  transfers between devices with their start and end apart: 5, of which 5 were waited for; matrix products, arithmetic and copies ran while one was open for 10% of the time, Pallas kernels for 0%

profile of v1, /device:TPU:0, one launch (start us, length us, event | category | flops | bytes accessed | tf_op | source)
XLA Modules:
  0.0 306.1 jit_solution(3137798809151796645)
XLA Ops:
  6.5 0.7 convert_element_type.11
  7.3 0.3 copy-done
  7.6 14.7 %fusion.3 = f32[1024,8,128]{2,1,0:T(8,128)S(1)} fusion(bf16[1024,8,2048]{2,1,0:T(8,128)(2,1)} %param.6, bf16[2048,128]{1,0:T(8,128)(2,1)S(1)} %copy-done), kind=kOutput, calls=%fused_computation.6 | convolution fusion | flops 4294967296 | bytes 38273024 | tf_op jit(solution)/shard_map/dot_general | solution.py:9
  22.3 1.4 fusion
  23.7 0.0 all-reduce.7.cloned.1.call-start
  23.8 41.1 %all-reduce.5.cloned.1.call-done = f32[1024,128]{1,0:T(8,128)} async-done(((f32[1024,128]{1,0:T(8,128)}), f32[1024,128]{1,0:T(8,128)}) %all-reduce.5.cloned.1.call-update) | async-done | bytes 524304 | tf_op jit(solution)/shard_map/psum | solution.py:30
  64.9 0.0 all-reduce.9.cloned.1.call-start
  64.9 21.0 %all-reduce.7.cloned.1.call-done = f32[1024,128]{1,0:T(8,128)} async-done(((f32[1024,128]{1,0:T(8,128)}), f32[1024,128]{1,0:T(8,128)}) %all-reduce.7.cloned.1.call-update) | async-done | bytes 524304 | tf_op jit(solution)/shard_map/psum | solution.py:30
  85.9 2.8 fusion.13
  88.8 0.2 all-reduce.11.cloned.1.call-start
  89.0 42.7 %all-reduce.9.cloned.1.call-done = f32[128,128]{0,1:T(8,128)} async-done(((f32[128,128]{0,1:T(8,128)}), f32[128,128]{0,1:T(8,128)}) %all-reduce.9.cloned.1.call-update) | async-done | bytes 65552 | tf_op jit(solution)/shard_map/psum | solution.py:32
  131.7 0.9 copy.6
  132.7 0.9 fusion.10
  133.5 11.7 %cholesky.44 = f32[128,128]{1,0:T(8,128)S(1)} custom-call(f32[128,128]{1,0:T(8,128)S(1)} %fusion.10), custom_call_target="Cholesky" | custom-call | tf_op jit(solution)/shard_map/jit(cholesky)/cholesky | solution.py:23
  145.3 0.6 compare_reduce_fusion.1
  145.9 0.7 fusion.5
  146.6 9.8 %custom-call.6 = f32[1,128,128]{1,2,0:T(8,128)S(1)} custom-call(f32[1,128,128]{2,1,0:T(8,128)S(1)} %fusion.5), custom_call_target="InvertDiagBlocksLowerTriangular" | custom-call | tf_op jit(solution)/shard_map/jit(_solve_triangular)/triangular_solve | solution.py:24
  156.4 1.7 fusion.1
  158.1 1.2 fusion.14
  159.3 0.0 reduce-scatter.2.cloned.1.call-start
  159.4 30.1 %copy.13 = bf16[128,8,8,2048]{3,1,2,0:T(8,128)(2,1)} copy(bf16[128,8,8,2048]{3,2,1,0:T(8,128)(2,1)} %bitcast.37) | data formatting | bytes 67108864
  189.4 11.6 %all-reduce.11.cloned.1.call-done = f32[128,128]{0,1:T(8,128)} async-done(((f32[128,128]{0,1:T(8,128)}), f32[128,128]{0,1:T(8,128)}) %all-reduce.11.cloned.1.call-update) | async-done | bytes 65552 | tf_op jit(solution)/shard_map/psum | solution.py:32
  201.0 0.9 copy.8
  201.9 0.9 fusion.8
  202.8 11.7 %cholesky.55 = f32[128,128]{1,0:T(8,128)S(1)} custom-call(f32[128,128]{1,0:T(8,128)S(1)} %fusion.8), custom_call_target="Cholesky" | custom-call | tf_op jit(solution)/shard_map/jit(cholesky)/cholesky | solution.py:23
  214.5 0.6 compare_reduce_fusion
  215.2 0.7 fusion.6
  215.8 9.8 %custom-call.7 = f32[1,128,128]{1,2,0:T(8,128)S(1)} custom-call(f32[1,128,128]{2,1,0:T(8,128)S(1)} %fusion.6), custom_call_target="InvertDiagBlocksLowerTriangular" | custom-call | tf_op jit(solution)/shard_map/jit(_solve_triangular)/triangular_solve | solution.py:24
  225.6 0.6 convolution_convert_fusion.1
  226.3 17.2 %convolution_convert_fusion = bf16[128,16384]{1,0:T(8,128)(2,1)} fusion(bf16[128,1024]{1,0:T(8,128)(2,1)S(1)} %convolution_convert_fusion.1, bf16[1024,16384]{1,0:T(8,128)(2,1)} %bitcast.38), kind=kOutput, calls=%fused_computation | convolution fusion | flops 4297064448 | bytes 38010880 | tf_op jit(solution)/shard_map/dot_general | solution.py:39
  243.5 52.9 %reduce-scatter.2.cloned.1.call-done = bf16[32,16384]{1,0:T(8,128)(2,1)} async-done(((bf16[128,16384]{1,0:T(8,128)(2,1)}), bf16[32,16384]{1,0:T(8,128)(2,1)}) %reduce-scatter.2.cloned.1.call-update) | async-done | bytes 1048592 | tf_op jit(solution)/shard_map/reduce_scatter | solution.py:38
  296.4 3.2 %copy.14 = f32[4,8,8,2048]{3,2,1,0:T(8,128)} copy(bf16[4,8,8,2048]{3,1,2,0:T(8,128)(2,1)} %bitcast.39) | data formatting | bytes 3145728
  (11 shorter events, 0.2 us)
Async XLA Ops:
  6.5 1.1 copy-start
  6.5 58.3 %all-reduce.5.cloned.1.call-start = ((), (), s32[]{:S(2)}) async-start(), calls=%async_computation.1 | async-start | bytes 1048576 | tf_op jit(solution)/shard_map/psum | solution.py:30
  23.7 62.2 %all-reduce.7.cloned.1.call-start = ((), (), s32[]{:S(2)}) async-start(), calls=%async_computation.2 | async-start | bytes 1048576 | tf_op jit(solution)/shard_map/psum | solution.py:30
  64.9 66.9 %all-reduce.9.cloned.1.call-start = ((), (), s32[]{:S(2)}) async-start(), calls=%async_computation.3 | async-start | bytes 131072 | tf_op jit(solution)/shard_map/psum | solution.py:32
  88.8 112.2 %all-reduce.11.cloned.1.call-start = ((), (), s32[]{:S(2)}) async-start(), calls=%async_computation.4 | async-start | bytes 131072 | tf_op jit(solution)/shard_map/psum | solution.py:32
  159.3 137.0 %reduce-scatter.2.cloned.1.call-start = ((), (), s32[]{:S(2)}) async-start(), calls=%async_computation.5 | async-start | bytes 5242880 | tf_op jit(solution)/shard_map/reduce_scatter | solution.py:38
  226.3 73.2 %copy-start.1 = (bf16[2048,128]{1,0:T(8,128)(2,1)S(1)}, bf16[2048,128]{1,0:T(8,128)(2,1)}, u32[]{:S(2)}) copy-start(bf16[2048,128]{1,0:T(8,128)(2,1)} %param.7) | copy-start | bytes 1572868
Sparse Core Ops, SparseCore 0:
  23.8 40.9 all-reduce.4
  67.2 18.6 all-reduce.6
  89.0 42.6 all-reduce.8
  159.4 41.4 all-reduce.10
  243.6 52.6 reduce-scatter.1

commit v2 on v0

--- a/solution.py
+++ b/solution.py
@@ -29,7 +29,7 @@
     partial_value = local_sketch(tensor, factor_j, factor_k)
     basis = lax.psum(partial_value, ("ja", "ka"))
     for sweep in range(2):
-        gram = lax.psum(local_gram(basis), "ia")
+        gram = jnp.sum(lax.all_gather(local_gram(basis), "ia"), axis=0)
         basis = apply_factor(gram, basis)
     basis_half = basis.astype(jnp.bfloat16)
     flattened = tensor.reshape(rows, slices * columns)

time: 301 us -> 231 us (0.77)
  waiting for transfers between devices: 164 us -> 80.2 us
  blocking collectives: 0 us -> 18.3 us
    psum x2 -> x0, waiting for transfers between devices: 52.1 us -> none  [shards(): gram = lax.psum(local_gram(basis), 'ia')]
    psum x1, waiting for transfers between devices: 58.9 us -> 28.9 us  [shards(): basis = lax.psum(partial_value, ('ja', 'ka'))]
    all_gather x0 -> x2, blocking collectives: none -> 18.3 us  [shards(): gram = jnp.sum(lax.all_gather(local_gram(basis), 'ia'), axis=0)]
  transfers between devices with their start and end apart: 4 -> 2, of which waited for: 4 -> 2; matrix products, arithmetic and copies ran while one was open for 10% -> 13% of each run, Pallas kernels for 0% -> 0%
where the time goes in v2:
time: 231 us
  waiting for transfers between devices  80.2 us (35%)
  other arithmetic  47.9 us (21%)
  matrix products  37 us (16%)
  local copies, waits for them, and re-layouts  33.7 us (15%)
  blocking collectives  18.3 us (8%)
  between operations  13.5 us (6%)
    reduce_scatter x1, waiting for transfers between devices, shards(): lax.psum_scatter(lax.dot_general(basis_half, flattened, (((0,), (0,)), ((...  51.2 us
    unnamed x6, local copies, waits for them, and re-layouts  33.5 us
    psum x1, waiting for transfers between devices, shards(): basis = lax.psum(partial_value, ('ja', 'ka'))  28.9 us
    another operation x6, other arithmetic, apply_factor(): lower = jnp.linalg.cholesky(gram)  24.8 us
    another operation x4, other arithmetic, apply_factor(): return jax.scipy.linalg.solve_triangular(lower, basis.T, lower=True).T  20.9 us
    all_gather x2, blocking collectives, shards(): gram = jnp.sum(lax.all_gather(local_gram(basis), 'ia'), axis=0)  18.3 us
    dot_general x1, matrix products, shards(): lax.dot_general(basis_half, flattened, (((0,), (0,)), ((), ())), preferre...  17.2 us
    dot_general x1, matrix products, local_sketch(): jnp.dot(tensor.reshape(rows * slices, columns), factor_j, preferred_eleme...  14.7 us
  transfers between devices with their start and end apart: 2, of which 2 were waited for; matrix products, arithmetic and copies ran while one was open for 13% of the time, Pallas kernels for 0%

profile of v2, /device:TPU:0, one launch (start us, length us, event | category | flops | bytes accessed | tf_op | source)
XLA Modules:
  0.0 230.6 jit_solution(17668241740844972866)
XLA Ops:
  6.5 0.0 copy-start
  6.5 0.0 all-reduce.2.cloned.1.call-start
  6.5 0.7 convert_element_type.11
  7.3 0.3 copy-done
  7.6 14.7 %fusion.3 = f32[1024,8,128]{2,1,0:T(8,128)S(1)} fusion(bf16[1024,8,2048]{2,1,0:T(8,128)(2,1)} %param.6, bf16[2048,128]{1,0:T(8,128)(2,1)S(1)} %copy-done), kind=kOutput, calls=%fused_computation.6 | convolution fusion | flops 4294967296 | bytes 38273024 | tf_op jit(solution)/shard_map/dot_general | solution.py:9
  22.3 1.4 fusion
  23.7 0.0 all-reduce.2.cloned.1.call-update
  23.7 0.0 reduce-scatter.2.cloned.1.call-start
  23.8 30.1 %copy.12 = bf16[128,8,8,2048]{3,1,2,0:T(8,128)(2,1)} copy(bf16[128,8,8,2048]{3,2,1,0:T(8,128)(2,1)} %bitcast.39) | data formatting | bytes 67108864
  53.8 28.9 %all-reduce.2.cloned.1.call-done = f32[1024,128]{1,0:T(8,128)} async-done(((f32[1024,128]{1,0:T(8,128)}), f32[1024,128]{1,0:T(8,128)}) %all-reduce.2.cloned.1.call-update) | async-done | bytes 524304 | tf_op jit(solution)/shard_map/psum | solution.py:30
  82.7 2.2 fusion.13
  84.9 9.4 %all-gather = f32[512,128]{1,0:T(8,128)S(1)} all-gather(f32[128,128]{1,0:T(8,128)S(1)} %fusion.13), channel_id=2, replica_groups=mesh['ia'=4,'ja'=2,'ka'=4] {'ia'}, dimensions={0}, use_global_device_ids=true | all-gather | bytes 327680 | tf_op jit(solution)/shard_map/all_gather | solution.py:32
  94.4 0.1 copy.8
  94.5 11.7 %cholesky.44 = f32[128,128]{1,0:T(8,128)S(1)} custom-call(f32[128,128]{1,0:T(8,128)S(1)} %fusion.10), custom_call_target="Cholesky" | custom-call | tf_op jit(solution)/shard_map/jit(cholesky)/cholesky | solution.py:23
  106.2 0.6 compare_reduce_fusion.1
  106.9 0.7 fusion.5
  107.5 9.8 %custom-call.6 = f32[1,128,128]{1,2,0:T(8,128)S(1)} custom-call(f32[1,128,128]{2,1,0:T(8,128)S(1)} %fusion.5), custom_call_target="InvertDiagBlocksLowerTriangular" | custom-call | tf_op jit(solution)/shard_map/jit(_solve_triangular)/triangular_solve | solution.py:24
  117.3 1.7 fusion.1
  119.0 0.6 fusion.14
  119.6 8.9 %all-gather.1 = f32[512,128]{1,0:T(8,128)S(1)} all-gather(f32[128,128]{1,0:T(8,128)S(1)} %fusion.14), channel_id=3, replica_groups=mesh['ia'=4,'ja'=2,'ka'=4] {'ia'}, dimensions={0}, use_global_device_ids=true | all-gather | bytes 327680 | tf_op jit(solution)/shard_map/all_gather | solution.py:32
  128.5 0.1 copy.9
  128.7 11.7 %cholesky.55 = f32[128,128]{1,0:T(8,128)S(1)} custom-call(f32[128,128]{1,0:T(8,128)S(1)} %fusion.8), custom_call_target="Cholesky" | custom-call | tf_op jit(solution)/shard_map/jit(cholesky)/cholesky | solution.py:23
  140.4 0.6 compare_reduce_fusion
  141.1 0.7 fusion.6
  141.7 9.8 %custom-call.7 = f32[1,128,128]{1,2,0:T(8,128)S(1)} custom-call(f32[1,128,128]{2,1,0:T(8,128)S(1)} %fusion.6), custom_call_target="InvertDiagBlocksLowerTriangular" | custom-call | tf_op jit(solution)/shard_map/jit(_solve_triangular)/triangular_solve | solution.py:24
  151.5 0.6 convolution_convert_fusion.1
  152.2 0.0 copy-start.1
  152.2 17.2 %convolution_convert_fusion = bf16[128,16384]{1,0:T(8,128)(2,1)} fusion(bf16[128,1024]{1,0:T(8,128)(2,1)S(1)} %convolution_convert_fusion.1, bf16[1024,16384]{1,0:T(8,128)(2,1)} %bitcast.40), kind=kOutput, calls=%fused_computation | convolution fusion | flops 4297064448 | bytes 38010880 | tf_op jit(solution)/shard_map/dot_general | solution.py:39
  169.4 0.0 reduce-scatter.2.cloned.1.call-update
  169.4 51.2 %reduce-scatter.2.cloned.1.call-done = bf16[32,16384]{1,0:T(8,128)(2,1)} async-done(((bf16[128,16384]{1,0:T(8,128)(2,1)}), bf16[32,16384]{1,0:T(8,128)(2,1)}) %reduce-scatter.2.cloned.1.call-update) | async-done | bytes 1048592 | tf_op jit(solution)/shard_map/reduce_scatter | solution.py:38
  220.6 3.2 %copy.13 = f32[4,8,8,2048]{3,2,1,0:T(8,128)} copy(bf16[4,8,8,2048]{3,1,2,0:T(8,128)(2,1)} %bitcast.41) | data formatting | bytes 3145728
  223.8 0.0 copy-done.1
  (6 shorter events, 0.1 us)
Async XLA Ops:
  6.5 1.1 copy-start
  6.5 76.2 %all-reduce.2.cloned.1.call-start = ((), (), s32[]{:S(2)}) async-start(), calls=%async_computation.1 | async-start | bytes 1048576 | tf_op jit(solution)/shard_map/psum | solution.py:30
  23.7 196.9 %reduce-scatter.2.cloned.1.call-start = ((), (), s32[]{:S(2)}) async-start(), calls=%async_computation.2 | async-start | bytes 5242880 | tf_op jit(solution)/shard_map/reduce_scatter | solution.py:38
  152.2 71.6 %copy-start.1 = (bf16[2048,128]{1,0:T(8,128)(2,1)S(1)}, bf16[2048,128]{1,0:T(8,128)(2,1)}, u32[]{:S(2)}) copy-start(bf16[2048,128]{1,0:T(8,128)(2,1)} %param.7) | copy-start | bytes 1572868
Sparse Core Ops, SparseCore 0:
  23.8 58.8 all-reduce.1
  169.5 51.0 reduce-scatter.1
